TPU v7x, 32 devices: a whole 2x2x4 slice. The times are simulated.
32 devices in a mesh: ha: 8 (over y, x, core), wa: 4 (over z).
Axes of the slice: x: 2, y: 2, z: 4, core: 2. Of those that a mesh axis runs over, the one named last changes fastest.
Arguments:
- tokens: bfloat16 [128, 64, 256], P('ha', 'wa'), may hold values from -6 to 6
- gain_attn: float32 [256], replicated, may hold values from 0.25 to 1.75
- qkv_fine: bfloat16 [256, 768], replicated, may hold values from -0.375 to 0.375
- scale_fine: float32 [4], replicated, may hold values from 2 to 24
- out_fine: bfloat16 [256, 256], replicated, may hold values from -0.375 to 0.375
- gain_ffn: float32 [256], replicated, may hold values from 0.25 to 1.75
- ffn_in: bfloat16 [256, 1536], replicated, may hold values from -0.375 to 0.375
- ffn_out: bfloat16 [768, 256], replicated, may hold values from -0.21875 to 0.21875
- up_proj: bfloat16 [256, 1024], replicated, may hold values from -0.375 to 0.375
- gain_coarse: float32 [1024], replicated, may hold values from 0.25 to 1.75
- qkv_coarse: bfloat16 [1024, 3072], replicated, may hold values from -0.1875 to 0.1875
- scale_coarse: float32 [16], replicated, may hold values from 2 to 24
- out_coarse: bfloat16 [1024, 1024], replicated, may hold values from -0.1875 to 0.1875
Outputs:
- fine_out: bfloat16 [128, 64, 256], P('ha', 'wa')
- coarse_out: bfloat16 [8, 4, 1024], P('ha', 'wa')
All inputs are finite; a program needn't handle non-finite values.
Results may differ from a plain program's by a relative error of at most 0.03.
Values may be sent and summed in bfloat16 or wider, within the bound.
No kernel may reach another device: no remote copies, remote signals or barrier semaphores. Data moves between devices by JAX's collectives and lax.ppermute only.
A program may use at most 128 MiB of HBM per device.

v0:
```python
import functools

import jax
import jax.numpy as jnp
from jax import lax
from jax.experimental import pallas as pl
from jax.experimental.pallas import tpu as pltpu
from jax.sharding import PartitionSpec as P

HD = 64
RADIUS = 3
LOG2E = 1.4426950408889634
BIG = 2.0**30
BF = jnp.bfloat16
F32 = jnp.float32
MIB = 1 << 20


def rounded_up(value, step):
    return -(-value // step) * step


def dot(a, b):
    return jnp.dot(a, b, preferred_element_type=F32)


def dot_nt(a, b):
    return lax.dot_general(a, b, (((1,), (1,)), ((), ())), preferred_element_type=F32)


def dot_split(values, ones):
    high = values.astype(BF)
    low = (values - high.astype(F32)).astype(BF)
    return dot(high, ones) + dot(low, ones)


def same_head(rows, cols):
    shape = (rows, cols)
    left = lax.broadcasted_iota(jnp.int32, shape, 0) // HD
    right = lax.broadcasted_iota(jnp.int32, shape, 1) // HD
    return (left == right).astype(F32).astype(BF)


def head_norm(values, ones):
    return values * lax.rsqrt(dot_split(values * values, ones) * (1.0 / HD) + 1e-06)


def rms_norm(values, gain):
    mean = jnp.mean(values * values, -1, keepdims=True)
    return values * lax.rsqrt(mean + 1e-06) * gain


def copies_of(pairs, sems):
    return [pltpu.make_async_copy(src, dst, sems.at[i]) for i, (src, dst) in enumerate(pairs)]


def start_all(copies):
    for copy in copies:
        copy.start()


def wait_all(copies):
    for copy in copies:
        copy.wait()


def strip_kernel(rows, cols, axis, tok_hbm, across_ref, within_ref, sems):
    count, strip = rows * cols, RADIUS * cols
    odd = lax.axis_index(axis) % 2
    last = count - strip
    first = pl.multiple_of(odd * last, 16)
    second = pl.multiple_of((1 - odd) * last, 16)
    copies = copies_of(
        [
            (tok_hbm.at[pl.ds(first, strip), :], across_ref),
            (tok_hbm.at[pl.ds(second, strip), :], within_ref),
        ],
        sems,
    )
    start_all(copies)
    wait_all(copies)


def edge_kernel(rows, cols, axes, tok_ref, across_ref, within_ref, after_ref, across_out, within_out):
    height = rows + 2 * RADIUS
    strip = RADIUS * cols
    padded = across_out.shape[0]
    odd, odd_col = lax.axis_index(axes[0]) % 2, lax.axis_index(axes[1]) % 2
    block = jnp.concatenate([tok_ref[...], across_ref[...], within_ref[...]], 0)
    out = lax.broadcasted_iota(jnp.int32, (padded, 1), 0)
    src = lax.broadcasted_iota(jnp.int32, (padded, block.shape[0]), 1)
    row = ((out * 21846) >> 16) - RADIUS
    col = out - 3 * (row + RADIUS)
    above = rows * cols + strip * odd + RADIUS * cols
    below = rows * cols + strip * (1 - odd) - rows * cols
    first = row * cols + col + jnp.where(row < 0, above, jnp.where(row >= rows, below, 0))
    first = jnp.where(out < height * RADIUS, first, -2 * cols)
    far = cols - RADIUS
    pick = jnp.where(src == first + far * odd_col, 1.0, 0.0).astype(BF)
    across_out[...] = dot(pick, block).astype(BF)
    pick = jnp.where(src == first + far * (1 - odd_col), 1.0, 0.0).astype(BF)
    within_out[...] = dot(pick, block).astype(BF)


def column_copies(src, dst, start, blocks, sems):
    size = dst.shape[1] // blocks
    spans = [pl.ds(i * size, size) for i in range(blocks)]
    pairs = [(src.at[:, pl.ds(start + i * size, size)], dst.at[:, span]) for i, span in enumerate(spans)]
    return copies_of(pairs, sems), spans


def merge_columns(copies, spans, scaled, weight_ref, merged_ref):
    for copy, span in zip(copies, spans):
        copy.wait()
        merged_ref[:, span] = dot(scaled, weight_ref[:, span]).astype(BF)


def merge_kernel(after_ref, scaled_ref, qkv_hbm, merged_ref, weight_ref, sems):
    copies, spans = column_copies(qkv_hbm, weight_ref, weight_ref.shape[0], sems.shape[0], sems)
    start_all(copies)
    merge_columns(copies, spans, scaled_ref[...], weight_ref, merged_ref)


def half_lanes():
    return lax.broadcasted_iota(jnp.int32, (1, 2 * HD), 1) < HD


def mask_columns(rows, cols):
    place = lax.broadcasted_iota(jnp.int32, (1, 2 * HD), 1) % HD
    return place, place < rows, (place >= rows) & (place < rows + cols)


def query_columns(rows, cols):
    place, is_row, is_col = mask_columns(rows, cols)
    spot = lax.broadcasted_iota(jnp.int32, (rows * cols, 1), 0)
    hot = (is_row & (spot // cols == place)) | (is_col & (spot % cols == place - rows))
    return jnp.where(hot, 1.0, 0.0).astype(BF)


def key_columns(rows, cols, krow, kcol):
    place, is_row, is_col = mask_columns(rows, cols)
    far_row = jnp.abs(krow - place) > RADIUS
    far_col = jnp.abs(kcol - (place - rows)) > RADIUS
    return jnp.where((is_row & far_row) | (is_col & far_col), -BIG, 0.0).astype(BF)


def attend(head, query, key, value, query_mask, key_mask, factor):
    lanes = 2 * HD
    low = half_lanes()
    mine = low if head % 2 == 0 else ~low
    span = slice(head // 2 * lanes, (head // 2 + 1) * lanes)
    q = jnp.where(mine, query[:, span], query_mask)
    k = jnp.where(mine, key[:, span], key_mask)
    v = jnp.where(mine, value[:, span], jnp.ones((1, lanes), BF))
    weights = jnp.exp2(dot_nt(q, k) * (factor * (LOG2E / HD))).astype(BF)
    return dot(weights, v)


def own_kernel(rows, cols, heads, *refs):
    count = (len(refs) - 9) // 2
    ins, qkv_c_hbm, outs = refs[:count], refs[count], refs[count + 1 : 2 * count + 1]
    query_ref, acc_ref, scaled_ref, merged_ref, lanes_ref, weight_ref, sems, block_sems = refs[2 * count + 1 :]
    tok_ref, qkv_ref, gain_ref, scale_ref, up_ref, gain_c_ref, scale_c_ref = outs[:7]
    copies = copies_of(list(zip(ins, outs)), sems)
    blocks, spans = column_copies(qkv_c_hbm, weight_ref, 0, block_sems.shape[0], block_sems)
    start_all(copies[:7])
    start_all(blocks)
    start_all(copies[7:])
    width = heads * HD
    ones = same_head(width, width)
    query_mask = query_columns(rows, cols)
    spot = lax.broadcasted_iota(jnp.int32, (rows * cols, 1), 0)
    key_mask = key_columns(rows, cols, spot // cols, spot % cols)
    wait_all(copies[:4])
    normed = rms_norm(tok_ref[...].astype(F32), gain_ref[...]).astype(BF)
    query = head_norm(dot(normed, qkv_ref[:, :width]), ones).astype(BF)
    key = head_norm(dot(normed, qkv_ref[:, width : 2 * width]), ones).astype(BF)
    value = dot(normed, qkv_ref[:, 2 * width :]).astype(BF)
    query_ref[...] = query
    for head in range(heads):
        factor = scale_ref[0:1, head : head + 1]
        acc_ref[head] = attend(head, query, key, value, query_mask, key_mask, factor)
    wait_all(copies[4:7])
    lane = lax.broadcasted_iota(jnp.int32, lanes_ref.shape, 1) // HD
    lanes = jnp.zeros(lanes_ref.shape, F32)
    for head in range(scale_c_ref.shape[1]):
        lanes = jnp.where(lane == head, scale_c_ref[0:1, head : head + 1], lanes)
    lanes_ref[...] = lanes * (1.0 / HD)
    scaled = (up_ref[...].astype(F32) * gain_c_ref[...]).astype(BF)
    scaled_ref[...] = scaled
    merge_columns(blocks, spans, scaled, weight_ref, merged_ref)
    wait_all(copies[7:])


def fine_kernel(
    rows, cols, heads, axes,
    tok_ref, halo_refs, query_ref, acc_ref, gain_attn_ref, qkv_ref, scale_ref,
    out_ref, gain_ffn_ref, ffn_in_ref, ffn_out_ref, after_ref, out_c_hbm,
    fine_ref, pooled_ref, out_c_ref, sems,
):
    copies = copies_of([(out_c_hbm, out_c_ref)], sems)
    start_all(copies)
    strip = RADIUS * cols
    side = halo_refs[-1].shape[0]
    width = heads * HD
    total = 2 * strip + 2 * side
    row_axis, col_axis = axes
    row0 = lax.axis_index(row_axis) * rows
    col0 = lax.axis_index(col_axis) * cols
    grid_rows = lax.axis_size(row_axis) * rows
    grid_cols = lax.axis_size(col_axis) * cols

    halo = jnp.concatenate([ref[...] for ref in halo_refs], 0)
    normed = rms_norm(halo.astype(F32), gain_attn_ref[...]).astype(BF)
    ones = same_head(width, width)
    key = head_norm(dot(normed, qkv_ref[:, width : 2 * width]), ones).astype(BF)
    value = dot(normed, qkv_ref[:, 2 * width :]).astype(BF)

    odd, odd_col = lax.axis_index(row_axis) % 2, lax.axis_index(col_axis) % 2
    row_at = (odd * (rows + RADIUS) - RADIUS, (1 - odd) * (rows + RADIUS) - RADIUS)
    col_at = (odd_col * (cols + RADIUS) - RADIUS, (1 - odd_col) * (cols + RADIUS) - RADIUS)
    spot = lax.broadcasted_iota(jnp.int32, (total, 1), 0)
    past_first = spot - strip
    past_strips = past_first - strip
    past_third = past_strips - side
    strip_at = jnp.where(past_first >= 0, past_first, spot)
    side_at = jnp.where(past_third >= 0, past_third, past_strips)
    side_row = (side_at * 21846) >> 16
    in_strip = past_strips < 0
    krow = jnp.where(
        in_strip,
        strip_at // cols + jnp.where(past_first >= 0, row_at[1], row_at[0]),
        side_row - RADIUS,
    )
    kcol = jnp.where(
        in_strip,
        strip_at % cols,
        side_at - 3 * side_row + jnp.where(past_third >= 0, col_at[1], col_at[0]),
    )
    real = in_strip | (side_at < (rows + 2 * RADIUS) * RADIUS)
    real = real & (krow + row0 >= 0) & (krow + row0 < grid_rows)
    real = real & (kcol + col0 >= 0) & (kcol + col0 < grid_cols)
    key_mask = key_columns(rows, cols, jnp.where(real, krow, -1000), kcol)
    query_mask = query_columns(rows, cols)

    query = query_ref[...]
    low = half_lanes()
    parts = []
    for pair in range(heads // 2):
        sums = []
        for head in (2 * pair, 2 * pair + 1):
            factor = scale_ref[0:1, head : head + 1]
            sums.append(acc_ref[head] + attend(head, query, key, value, query_mask, key_mask, factor))
        top = jnp.where(low, sums[0], sums[1])
        bottom = pltpu.roll(jnp.where(low, sums[1], sums[0]), HD, 1)
        parts.append((top / bottom).astype(BF))
    attn = jnp.concatenate(parts, 1)

    h1 = (tok_ref[...].astype(F32) + dot(attn, out_ref[...])).astype(BF)
    h1_wide = h1.astype(F32)
    n2 = rms_norm(h1_wide, gain_ffn_ref[...]).astype(BF)
    hidden = ffn_out_ref.shape[0]
    gate = dot(n2, ffn_in_ref[:, :hidden])
    up = dot(n2, ffn_in_ref[:, hidden:])
    gated = (jax.nn.gelu(gate, approximate=True) * up).astype(BF)
    fine = (h1_wide + dot(gated, ffn_out_ref[...])).astype(BF)
    fine_ref[...] = fine
    pooled = jnp.mean(fine.astype(F32), 0, keepdims=True).astype(BF).astype(F32)
    for part in range(pooled_ref.shape[1]):
        pooled_ref[:, part, :] = jnp.broadcast_to(
            pooled[:, part * 128 : (part + 1) * 128], (pooled_ref.shape[0], 128)
        )
    wait_all(copies)


def coarse_kernel(
    axes, pooled_ref, up_ref, merged_query_ref, merged_ref, scale_ref, out_ref, fine_ref,
    coarse_out_ref, fine_hbm,
    query_ref, coarse_ref, sems,
):
    copies = copies_of([(fine_ref, fine_hbm)], sems)
    start_all(copies)
    width = out_ref.shape[0]
    row_axis, col_axis = axes
    mine = lax.axis_index(row_axis) * lax.axis_size(col_axis) + lax.axis_index(col_axis)
    pooled = jnp.concatenate([pooled_ref[:, part, :] for part in range(pooled_ref.shape[1])], 1).astype(BF)
    coarse = dot(pooled, up_ref[...]).astype(BF).astype(F32)
    coarse_ref[...] = coarse
    rms = lax.rsqrt(jnp.mean(coarse * coarse, -1, keepdims=True) + 1e-06)
    query_ref[...] = dot(pooled, merged_query_ref[...]) * rms
    key = dot(pooled, merged_ref[:, :width]) * rms
    value = dot(pooled, merged_ref[:, width:]) * rms
    query = query_ref[pl.ds(mine, 1), :]
    group = 4 * HD
    spans = [slice(at, at + group) for at in range(0, width, group)]
    tall = jnp.concatenate([key[:, span] for span in spans], 0)
    queries = [query[:, span] for span in spans]
    cross = jnp.concatenate([key[:, span] * q for span, q in zip(spans, queries)], 0)
    ones = same_head(group, group)
    query_norm = lax.rsqrt(dot_split(jnp.concatenate([q * q for q in queries], 0), ones) * (1.0 / HD) + 1e-06)
    key_norm = lax.rsqrt(dot_split(tall * tall, ones) * (1.0 / HD) + 1e-06)
    scores = dot_split(cross, ones) * key_norm
    count = key.shape[0]
    parts = []
    for at, span in enumerate(spans):
        factor = query_norm[at : at + 1] * scale_ref[:, span]
        expo = jnp.exp(scores[at * count : (at + 1) * count] * factor)
        total = jnp.sum(expo, 0, keepdims=True)
        parts.append(jnp.sum(expo * value[:, span], 0, keepdims=True) / total)
    cattn = jnp.concatenate(parts, 1).astype(BF)
    coarse_out_ref[...] = (coarse_ref[pl.ds(mine, 1), :] + dot(cattn, out_ref[...])).astype(BF)
    wait_all(copies)


def vmem(count):
    return [pl.BlockSpec(memory_space=pltpu.VMEM)] * count


def anywhere(count):
    return [pl.BlockSpec(memory_space=pl.ANY)] * count


def in_vmem(arrays):
    return [pltpu.with_memory_space_constraint(array, pltpu.VMEM) for array in arrays]


def in_hbm(arrays):
    return [pltpu.with_memory_space_constraint(array, pltpu.HBM) for array in arrays]


def shards(
    tokens, gain_attn, qkv_fine, scale_fine, out_fine, gain_ffn, ffn_in, ffn_out,
    up_proj, gain_coarse, qkv_coarse, scale_coarse, out_coarse,
):
    rows, cols, width = tokens.shape
    count = rows * cols
    strip = RADIUS * cols
    side = rounded_up((rows + 2 * RADIUS) * RADIUS, 16)
    heads = width // HD
    width_c = out_coarse.shape[0]
    devices = lax.axis_size("ha") * lax.axis_size("wa")
    axes = ("ha", "wa")
    params = pltpu.CompilerParams(vmem_limit_bytes=16 * MIB)

    def swapped(array, axis, first):
        pairs = [(i, i + 1) for i in range(first, lax.axis_size(axis) - 1, 2)]
        return lax.ppermute(array, axis, pairs + [(j, i) for i, j in pairs])

    flat = tokens.reshape(count, width)
    across, within = pl.pallas_call(
        functools.partial(strip_kernel, rows, cols, "ha"),
        out_shape=[pltpu.VMEM((strip, width), BF)] * 2,
        in_specs=anywhere(1),
        out_specs=vmem(2),
        scratch_shapes=[pltpu.SemaphoreType.DMA((2,))],
        compiler_params=params,
        name="strips",
    )(*in_hbm([flat]))
    across = swapped(across, "ha", 1)
    within = swapped(within, "ha", 0)

    weights = [
        flat, qkv_fine, gain_attn.reshape(1, -1), scale_fine.reshape(1, -1),
        up_proj, gain_coarse.reshape(1, -1), scale_coarse.reshape(1, -1),
        out_fine, gain_ffn.reshape(1, -1), ffn_in, ffn_out,
    ]
    *weights, query, acc, scaled, merged_query, scale_lanes = pl.pallas_call(
        functools.partial(own_kernel, rows, cols, heads),
        out_shape=[pltpu.VMEM(array.shape, array.dtype) for array in weights]
        + [
            pltpu.VMEM((count, width), BF),
            pltpu.VMEM((heads, count, 2 * HD), F32),
            pltpu.VMEM((width, width_c), BF),
            pltpu.VMEM((width, width_c), BF),
            pltpu.VMEM((1, width_c), F32),
        ],
        in_specs=anywhere(len(weights) + 1),
        out_specs=vmem(len(weights) + 5),
        scratch_shapes=[
            pltpu.VMEM((width_c, width_c), BF),
            pltpu.SemaphoreType.DMA((len(weights),)),
            pltpu.SemaphoreType.DMA((2,)),
        ],
        compiler_params=params,
        cost_estimate=pl.CostEstimate(
            flops=2 * count * width * (3 * width + 2 * count) + 2 * width * width_c * width_c,
            bytes_accessed=8 * MIB,
            transcendentals=0,
        ),
        name="own",
    )(*in_hbm(weights + [qkv_coarse]))
    tok_v, qkv_v, gain_attn_v, scale_v, up_v = weights[:5]
    out_v, gain_ffn_v, ffn_in_v, ffn_out_v = weights[7:]

    across_edge, within_edge = pl.pallas_call(
        functools.partial(edge_kernel, rows, cols, axes),
        out_shape=[pltpu.VMEM((side, width), BF)] * 2,
        in_specs=vmem(4),
        out_specs=vmem(2),
        compiler_params=params,
        name="edges",
    )(*in_vmem([tok_v, across, within, query]))
    across_side = swapped(across_edge, "wa", 1)
    within_side = swapped(within_edge, "wa", 0)

    merged = pl.pallas_call(
        merge_kernel,
        out_shape=pltpu.VMEM((width, 2 * width_c), BF),
        in_specs=vmem(2) + anywhere(1),
        out_specs=vmem(1)[0],
        scratch_shapes=[pltpu.VMEM((width_c, 2 * width_c), BF), pltpu.SemaphoreType.DMA((4,))],
        compiler_params=params,
        cost_estimate=pl.CostEstimate(
            flops=4 * width * width_c * width_c, bytes_accessed=6 * MIB, transcendentals=0
        ),
        name="merge",
    )(*in_vmem([within_edge, scaled]), *in_hbm([qkv_coarse]))

    def fine_body(tok_ref, *refs):
        fine_kernel(rows, cols, heads, axes, tok_ref, refs[:4], *refs[4:])

    fine, pooled, out_c_v = pl.pallas_call(
        fine_body,
        out_shape=[
            pltpu.VMEM((count, width), BF),
            pltpu.VMEM((devices, width // 128, 128), F32),
            pltpu.VMEM(out_coarse.shape, BF),
        ],
        in_specs=vmem(15) + anywhere(1),
        out_specs=vmem(3),
        scratch_shapes=[pltpu.SemaphoreType.DMA((1,))],
        compiler_params=params,
        name="fine",
    )(
        *in_vmem(
            [tok_v, across, within, across_side, within_side, query, acc, gain_attn_v, qkv_v, scale_v]
            + [out_v, gain_ffn_v, ffn_in_v, ffn_out_v, merged]
        ),
        *in_hbm([out_coarse]),
    )

    every = lax.all_to_all(pooled, axes, split_axis=0, concat_axis=0, tiled=True)
    coarse_out, fine = pl.pallas_call(
        functools.partial(coarse_kernel, axes),
        out_shape=[
            jax.ShapeDtypeStruct((1, width_c), BF),
            jax.ShapeDtypeStruct((count, width), BF),
        ],
        in_specs=vmem(7),
        out_specs=vmem(1) + anywhere(1),
        scratch_shapes=[pltpu.VMEM((devices, width_c), F32)] * 2 + [pltpu.SemaphoreType.DMA((1,))],
        compiler_params=params,
        name="coarse",
    )(*in_vmem([every, up_v, merged_query, merged, scale_lanes, out_c_v, fine]))
    return fine.reshape(rows, cols, width), coarse_out.reshape(1, 1, width_c)


def solution(mesh):
    return jax.shard_map(
        shards,
        mesh=mesh,
        in_specs=(P("ha", "wa", None), P(), P(), P(), P(), P(), P(), P(), P(), P(), P(), P(), P()),
        out_specs=(P("ha", "wa", None), P("ha", "wa", None)),
        check_vma=False,
    )
```

profile of v0, /device:TPU:0, one launch (start us, length us, event | category | flops | bytes accessed | tf_op | source)
XLA Modules:
  0.0 32.2 jit_solution(13703426874487131509)
XLA Ops:
  0.6 0.8 %strips.1 = (bf16[48,256]{1,0:T(8,128)(2,1)S(1)}, bf16[48,256]{1,0:T(8,128)(2,1)S(1)}) custom-call(bf16[256,256]{1,0:T(8,128)(2,1)} %bitcast.8), custom_call_target="tpu_custom_call" | custom-call | tf_op jit(solution)/shard_map/strips/pallas_call | solution.py:350
  1.4 0.7 %collective-permute-start = (bf16[48,256]{1,0:T(8,128)(2,1)S(1)}, bf16[48,256]{1,0:T(8,128)(2,1)S(1)}, u32[]{:S(2)}, u32[]{:S(2)}) collective-permute-start(bf16[48,256]{1,0:T(8,128)(2,1)S(1)} %get-tuple-element.26), channel_id=1, source_target_pairs={{4,8},{12,16},{20,24},{8,4},{16,12},{24,20},{5,9},{13,17},{21,25},... | collective-permute-start | bytes 73736 | tf_op jit(solution)/shard_map/ppermute | solution.py:347
  2.1 4.4 %collective-permute-start.1 = (bf16[48,256]{1,0:T(8,128)(2,1)S(1)}, bf16[48,256]{1,0:T(8,128)(2,1)S(1)}, u32[]{:S(2)}, u32[]{:S(2)}) collective-permute-start(bf16[48,256]{1,0:T(8,128)(2,1)S(1)} %get-tuple-element.27), channel_id=1, source_target_pairs={{0,4},{8,12},{16,20},{24,28},{4,0},{12,8},{20,16},{28,24},{1,5},{9... | collective-permute-start | bytes 73736 | tf_op jit(solution)/shard_map/ppermute | solution.py:347
  6.5 4.0 %own.1 = (bf16[256,256]{1,0:T(8,128)(2,1)S(1)}, bf16[256,768]{1,0:T(8,128)(2,1)S(1)}, f32[1,256]{1,0:T(1,128)S(1)}, f32[1,4]{1,0:T(1,128)S(1)}, bf16[256,1024]{1...) custom-call(bf16[256,256]{1,0:T(8,128)(2,1)} %bitcast.9, ...), custom_call_target="tpu_custom_call" | custom-call | flops 704643072 | bytes 8388608 | tf_op jit(solution)/shard_map/own/pallas_call | solution.py:367
  10.5 0.0 collective-permute-done.across_ref.refs_0_
  10.5 0.0 collective-permute-done.1.within_ref.refs_1_
  10.5 0.2 edges.1
  10.7 0.7 %collective-permute-start.2 = (bf16[80,256]{1,0:T(8,128)(2,1)S(1)}, bf16[80,256]{1,0:T(8,128)(2,1)S(1)}, u32[]{:S(2)}, u32[]{:S(2)}) collective-permute-start(bf16[80,256]{1,0:T(8,128)(2,1)S(1)} %get-tuple-element.29), channel_id=1, source_target_pairs={{1,2},{2,1},{5,6},{6,5},{9,10},{10,9},{13,14},{14,13},{17,18},{18,... | collective-permute-start | bytes 122888 | tf_op jit(solution)/shard_map/ppermute | solution.py:347
  11.3 4.5 %collective-permute-start.3 = (bf16[80,256]{1,0:T(8,128)(2,1)S(1)}, bf16[80,256]{1,0:T(8,128)(2,1)S(1)}, u32[]{:S(2)}, u32[]{:S(2)}) collective-permute-start(bf16[80,256]{1,0:T(8,128)(2,1)S(1)} %get-tuple-element.30.after_ref), channel_id=1, source_target_pairs={{0,1},{2,3},{1,0},{3,2},{4,5},{6,7},{5,4},{7,6},{8,9},{10,11},{9,8... | collective-permute-start | bytes 122888 | tf_op jit(solution)/shard_map/ppermute | solution.py:347
  15.8 3.0 %merge.1.refs_13_.merged_ref = bf16[256,2048]{1,0:T(8,128)(2,1)S(1)} custom-call(bf16[80,256]{1,0:T(8,128)(2,1)S(1)} %get-tuple-element.30.after_ref, bf16[256,1024]{1,0:T(8,128)(2,1)S(1)} %get-tuple-element.39.scaled_ref, bf16[1024,3072]{1,0:T(8,128)(2,1)} %qkv_hbm.1), custom_call_target="tpu_custom_call" | custom-call | flops 1073741824 | bytes 6291456 | tf_op jit(solution)/shard_map/merge/pallas_call | solution.py:406
  18.8 0.0 collective-permute-done.2.refs_2_
  18.9 0.0 collective-permute-done.3.refs_3_
  18.9 1.9 %fine.1 = (bf16[256,256]{1,0:T(8,128)(2,1)S(1)}, f32[32,2,128]{2,1,0:T(2,128)S(1)}, bf16[1024,1024]{1,0:T(8,128)(2,1)S(1)}) custom-call(bf16[256,256]{1,0:T(8,128)(2,1)S(1)} %get-tuple-element.25.tok_ref, bf16[48,256]{1,0:T(8,128)(2,1)S(1)} %collective-permute-done.across_ref.refs_0_, bf16[48,256]{1,0:T(8,128)(2,1)S(1)} %collective-permute-done.1.within_ref.refs_1_, ...), custom_call_target="tpu_custom_call" | custom-call | tf_op jit(solution)/shard_map/fine/pallas_call | solution.py:422
  20.8 9.8 %all_to_all.5.pooled_ref = f32[32,2,128]{2,1,0:T(2,128)S(1)} all-to-all(f32[32,2,128]{2,1,0:T(2,128)S(1)} %get-tuple-element.40), channel_id=1, replica_groups=mesh['ha'=8,'wa'=4] {'ha','wa'}, dimensions={0} | all-to-all | bytes 65536 | tf_op jit(solution)/shard_map/all_to_all | solution.py:442
  30.5 1.7 %coarse.1 = (bf16[1,1024]{1,0:T(2,128)(2,1)}, bf16[256,256]{1,0:T(8,128)(2,1)}) custom-call(f32[32,2,128]{2,1,0:T(2,128)S(1)} %all_to_all.5.pooled_ref, bf16[256,1024]{1,0:T(8,128)(2,1)S(1)} %get-tuple-element.41.up_ref, bf16[256,1024]{1,0:T(8,128)(2,1)S(1)} %get-tuple-element.42.merged_query_ref, bf16[256,2048]{1,0:T(8,128)(2,1)S(1)} %merge.1.refs_13_.merged_ref, ...), custom_call_target="tpu_custom_call" | custom-call | tf_op jit(solution)/shard_map/coarse/pallas_call | solution.py:443
Async XLA Ops:
  1.4 9.0 %collective-permute-start = (bf16[48,256]{1,0:T(8,128)(2,1)S(1)}, bf16[48,256]{1,0:T(8,128)(2,1)S(1)}, u32[]{:S(2)}, u32[]{:S(2)}) collective-permute-start(bf16[48,256]{1,0:T(8,128)(2,1)S(1)} %get-tuple-element.26), channel_id=1, source_target_pairs={{4,8},{12,16},{20,24},{8,4},{16,12},{24,20},{5,9},{13,17},{21,25},... | collective-permute-start | bytes 73736 | tf_op jit(solution)/shard_map/ppermute | solution.py:347
  2.1 8.4 %collective-permute-start.1 = (bf16[48,256]{1,0:T(8,128)(2,1)S(1)}, bf16[48,256]{1,0:T(8,128)(2,1)S(1)}, u32[]{:S(2)}, u32[]{:S(2)}) collective-permute-start(bf16[48,256]{1,0:T(8,128)(2,1)S(1)} %get-tuple-element.27), channel_id=1, source_target_pairs={{0,4},{8,12},{16,20},{24,28},{4,0},{12,8},{20,16},{28,24},{1,5},{9... | collective-permute-start | bytes 73736 | tf_op jit(solution)/shard_map/ppermute | solution.py:347
  10.7 8.2 %collective-permute-start.2 = (bf16[80,256]{1,0:T(8,128)(2,1)S(1)}, bf16[80,256]{1,0:T(8,128)(2,1)S(1)}, u32[]{:S(2)}, u32[]{:S(2)}) collective-permute-start(bf16[80,256]{1,0:T(8,128)(2,1)S(1)} %get-tuple-element.29), channel_id=1, source_target_pairs={{1,2},{2,1},{5,6},{6,5},{9,10},{10,9},{13,14},{14,13},{17,18},{18,... | collective-permute-start | bytes 122888 | tf_op jit(solution)/shard_map/ppermute | solution.py:347
  11.3 7.5 %collective-permute-start.3 = (bf16[80,256]{1,0:T(8,128)(2,1)S(1)}, bf16[80,256]{1,0:T(8,128)(2,1)S(1)}, u32[]{:S(2)}, u32[]{:S(2)}) collective-permute-start(bf16[80,256]{1,0:T(8,128)(2,1)S(1)} %get-tuple-element.30.after_ref), channel_id=1, source_target_pairs={{0,1},{2,3},{1,0},{3,2},{4,5},{6,7},{5,4},{7,6},{8,9},{10,11},{9,8... | collective-permute-start | bytes 122888 | tf_op jit(solution)/shard_map/ppermute | solution.py:347
where the time goes:
time: 32.4 us; the launch traced here: 32.2 us
  Pallas kernels  11.6 us (36%)
  starting transfers between devices  10.2 us (31%)
  blocking collectives  9.77 us (30%)
  between operations  0.72 us (2%)
    ppermute x4, starting transfers between devices, swapped(): return lax.ppermute(array, axis, pairs + [(j, i) for i, j in pairs])  10.2 us
    all_to_all x1, blocking collectives, shards(): lax.all_to_all(pooled, axes, split_axis=0, concat_axis=0, tiled=True)  9.77 us
    pallas_call x1, Pallas kernels, shards(): pl.pallas_call(functools.partial(own_kernel, rows, cols, heads), out_shap...  3.98 us
    pallas_call x1, Pallas kernels, shards(): pl.pallas_call(merge_kernel, out_shape=pltpu.VMEM((width, 2 * width_c), B...  3.03 us
    pallas_call x1, Pallas kernels, shards(): pl.pallas_call(fine_body, out_shape=[pltpu.VMEM((count, width), BF), pltp...  1.91 us
    pallas_call x1, Pallas kernels, shards(): pl.pallas_call(functools.partial(coarse_kernel, axes), out_shape=[jax.Sha...  1.67 us
    pallas_call x1, Pallas kernels, shards(): pl.pallas_call(functools.partial(strip_kernel, rows, cols, 'ha'), out_sha...  0.79 us
  transfers between devices with their start and end apart: 4, of which 0 were waited for; matrix products, arithmetic and copies ran while one was open for 0% of the time, Pallas kernels for 22%

commit v1 on v0

--- a/solution.py
+++ b/solution.py
@@ -109,16 +109,43 @@
     return copies_of(pairs, sems), spans
 
 
-def merge_columns(copies, spans, scaled, weight_ref, merged_ref):
+def merge_kernel(after_ref, up_ref, gain_ref, qkv_hbm, merged_ref, weight_ref, sems):
+    copies, spans = column_copies(qkv_hbm, weight_ref, weight_ref.shape[0], sems.shape[0], sems)
+    start_all(copies)
+    scaled = (up_ref[...].astype(F32) * gain_ref[...]).astype(BF)
     for copy, span in zip(copies, spans):
         copy.wait()
         merged_ref[:, span] = dot(scaled, weight_ref[:, span]).astype(BF)
 
 
-def merge_kernel(after_ref, scaled_ref, qkv_hbm, merged_ref, weight_ref, sems):
-    copies, spans = column_copies(qkv_hbm, weight_ref, weight_ref.shape[0], sems.shape[0], sems)
-    start_all(copies)
-    merge_columns(copies, spans, scaled_ref[...], weight_ref, merged_ref)
+def lane_scales(scale_ref, width):
+    lane = lax.broadcasted_iota(jnp.int32, (1, width), 1) // HD
+    scales = jnp.zeros((1, width), F32)
+    for head in range(scale_ref.shape[1]):
+        scales = jnp.where(lane == head, scale_ref[0:1, head : head + 1], scales)
+    return scales
+
+
+def query_kernel(pooled_ref, up_ref, gain_ref, scale_ref, qkv_hbm, rows_hbm, weight_ref, rows_ref, sems, out_sems):
+    width = weight_ref.shape[0]
+    copies, spans = column_copies(qkv_hbm, weight_ref, 0, sems.shape[0], sems)
+    start_all(copies)
+    count = min(8, pooled_ref.shape[0])
+    pooled = jnp.concatenate([pooled_ref[:count, part, :] for part in range(pooled_ref.shape[1])], 1).astype(BF)
+    coarse = dot(pooled, up_ref[...]).astype(BF).astype(F32)
+    normed = rms_norm(coarse, gain_ref[...]).astype(BF)
+    scales = lane_scales(scale_ref, width) * (1.0 / HD)
+    group = 4 * HD
+    ones = same_head(group, group)
+    rows_ref[1:2, :] = coarse[0:1]
+    wait_all(copies)
+    for at in range(0, width, group):
+        span = slice(at, at + group)
+        query = head_norm(dot(normed, weight_ref[:, span]), ones)
+        rows_ref[0:1, span] = query[0:1] * scales[:, span]
+    out = copies_of([(rows_ref, rows_hbm)], out_sems)
+    start_all(out)
+    wait_all(out)
 
 
 def half_lanes():
@@ -157,15 +184,11 @@
 
 
 def own_kernel(rows, cols, heads, *refs):
-    count = (len(refs) - 9) // 2
-    ins, qkv_c_hbm, outs = refs[:count], refs[count], refs[count + 1 : 2 * count + 1]
-    query_ref, acc_ref, scaled_ref, merged_ref, lanes_ref, weight_ref, sems, block_sems = refs[2 * count + 1 :]
-    tok_ref, qkv_ref, gain_ref, scale_ref, up_ref, gain_c_ref, scale_c_ref = outs[:7]
-    copies = copies_of(list(zip(ins, outs)), sems)
-    blocks, spans = column_copies(qkv_c_hbm, weight_ref, 0, block_sems.shape[0], block_sems)
-    start_all(copies[:7])
-    start_all(blocks)
-    start_all(copies[7:])
+    count = (len(refs) - 3) // 2
+    outs, (query_ref, acc_ref, sems) = refs[count : 2 * count], refs[2 * count :]
+    tok_ref, qkv_ref, gain_ref, scale_ref = outs[:4]
+    copies = copies_of(list(zip(refs[:count], outs)), sems)
+    start_all(copies)
     width = heads * HD
     ones = same_head(width, width)
     query_mask = query_columns(rows, cols)
@@ -180,16 +203,7 @@
     for head in range(heads):
         factor = scale_ref[0:1, head : head + 1]
         acc_ref[head] = attend(head, query, key, value, query_mask, key_mask, factor)
-    wait_all(copies[4:7])
-    lane = lax.broadcasted_iota(jnp.int32, lanes_ref.shape, 1) // HD
-    lanes = jnp.zeros(lanes_ref.shape, F32)
-    for head in range(scale_c_ref.shape[1]):
-        lanes = jnp.where(lane == head, scale_c_ref[0:1, head : head + 1], lanes)
-    lanes_ref[...] = lanes * (1.0 / HD)
-    scaled = (up_ref[...].astype(F32) * gain_c_ref[...]).astype(BF)
-    scaled_ref[...] = scaled
-    merge_columns(blocks, spans, scaled, weight_ref, merged_ref)
-    wait_all(copies[7:])
+    wait_all(copies[4:])
 
 
 def fine_kernel(
@@ -274,42 +288,36 @@
 
 
 def coarse_kernel(
-    axes, pooled_ref, up_ref, merged_query_ref, merged_ref, scale_ref, out_ref, fine_ref,
+    pooled_ref, up_ref, merged_ref, out_ref, fine_ref, rows_hbm,
     coarse_out_ref, fine_hbm,
-    query_ref, coarse_ref, sems,
+    rows_ref, sems,
 ):
-    copies = copies_of([(fine_ref, fine_hbm)], sems)
+    copies = copies_of([(rows_hbm, rows_ref), (fine_ref, fine_hbm)], sems)
     start_all(copies)
     width = out_ref.shape[0]
-    row_axis, col_axis = axes
-    mine = lax.axis_index(row_axis) * lax.axis_size(col_axis) + lax.axis_index(col_axis)
     pooled = jnp.concatenate([pooled_ref[:, part, :] for part in range(pooled_ref.shape[1])], 1).astype(BF)
     coarse = dot(pooled, up_ref[...]).astype(BF).astype(F32)
-    coarse_ref[...] = coarse
     rms = lax.rsqrt(jnp.mean(coarse * coarse, -1, keepdims=True) + 1e-06)
-    query_ref[...] = dot(pooled, merged_query_ref[...]) * rms
     key = dot(pooled, merged_ref[:, :width]) * rms
     value = dot(pooled, merged_ref[:, width:]) * rms
-    query = query_ref[pl.ds(mine, 1), :]
     group = 4 * HD
     spans = [slice(at, at + group) for at in range(0, width, group)]
     tall = jnp.concatenate([key[:, span] for span in spans], 0)
-    queries = [query[:, span] for span in spans]
-    cross = jnp.concatenate([key[:, span] * q for span, q in zip(spans, queries)], 0)
     ones = same_head(group, group)
-    query_norm = lax.rsqrt(dot_split(jnp.concatenate([q * q for q in queries], 0), ones) * (1.0 / HD) + 1e-06)
+    copies[0].wait()
+    query = rows_ref[0:1, :]
+    cross = jnp.concatenate([key[:, span] * query[:, span] for span in spans], 0)
     key_norm = lax.rsqrt(dot_split(tall * tall, ones) * (1.0 / HD) + 1e-06)
     scores = dot_split(cross, ones) * key_norm
     count = key.shape[0]
     parts = []
     for at, span in enumerate(spans):
-        factor = query_norm[at : at + 1] * scale_ref[:, span]
-        expo = jnp.exp(scores[at * count : (at + 1) * count] * factor)
+        expo = jnp.exp(scores[at * count : (at + 1) * count])
         total = jnp.sum(expo, 0, keepdims=True)
         parts.append(jnp.sum(expo * value[:, span], 0, keepdims=True) / total)
     cattn = jnp.concatenate(parts, 1).astype(BF)
-    coarse_out_ref[...] = (coarse_ref[pl.ds(mine, 1), :] + dot(cattn, out_ref[...])).astype(BF)
-    wait_all(copies)
+    coarse_out_ref[...] = (rows_ref[1:2, :] + dot(cattn, out_ref[...])).astype(BF)
+    copies[1].wait()
 
 
 def vmem(count):
@@ -364,32 +372,20 @@
         up_proj, gain_coarse.reshape(1, -1), scale_coarse.reshape(1, -1),
         out_fine, gain_ffn.reshape(1, -1), ffn_in, ffn_out,
     ]
-    *weights, query, acc, scaled, merged_query, scale_lanes = pl.pallas_call(
+    *weights, query, acc = pl.pallas_call(
         functools.partial(own_kernel, rows, cols, heads),
         out_shape=[pltpu.VMEM(array.shape, array.dtype) for array in weights]
-        + [
-            pltpu.VMEM((count, width), BF),
-            pltpu.VMEM((heads, count, 2 * HD), F32),
-            pltpu.VMEM((width, width_c), BF),
-            pltpu.VMEM((width, width_c), BF),
-            pltpu.VMEM((1, width_c), F32),
-        ],
-        in_specs=anywhere(len(weights) + 1),
-        out_specs=vmem(len(weights) + 5),
-        scratch_shapes=[
-            pltpu.VMEM((width_c, width_c), BF),
-            pltpu.SemaphoreType.DMA((len(weights),)),
-            pltpu.SemaphoreType.DMA((2,)),
-        ],
+        + [pltpu.VMEM((count, width), BF), pltpu.VMEM((heads, count, 2 * HD), F32)],
+        in_specs=anywhere(len(weights)),
+        out_specs=vmem(len(weights) + 2),
+        scratch_shapes=[pltpu.SemaphoreType.DMA((len(weights),))],
         compiler_params=params,
         cost_estimate=pl.CostEstimate(
-            flops=2 * count * width * (3 * width + 2 * count) + 2 * width * width_c * width_c,
-            bytes_accessed=8 * MIB,
-            transcendentals=0,
+            flops=2 * count * width * (3 * width + 2 * count), bytes_accessed=4 * MIB, transcendentals=0
         ),
         name="own",
-    )(*in_hbm(weights + [qkv_coarse]))
-    tok_v, qkv_v, gain_attn_v, scale_v, up_v = weights[:5]
+    )(*in_hbm(weights))
+    tok_v, qkv_v, gain_attn_v, scale_v, up_v, gain_c_v, scale_c_v = weights[:7]
     out_v, gain_ffn_v, ffn_in_v, ffn_out_v = weights[7:]
 
     across_edge, within_edge = pl.pallas_call(
@@ -406,7 +402,7 @@
     merged = pl.pallas_call(
         merge_kernel,
         out_shape=pltpu.VMEM((width, 2 * width_c), BF),
-        in_specs=vmem(2) + anywhere(1),
+        in_specs=vmem(3) + anywhere(1),
         out_specs=vmem(1)[0],
         scratch_shapes=[pltpu.VMEM((width_c, 2 * width_c), BF), pltpu.SemaphoreType.DMA((4,))],
         compiler_params=params,
@@ -414,7 +410,7 @@
             flops=4 * width * width_c * width_c, bytes_accessed=6 * MIB, transcendentals=0
         ),
         name="merge",
-    )(*in_vmem([within_edge, scaled]), *in_hbm([qkv_coarse]))
+    )(*in_vmem([within_edge, up_v, gain_c_v]), *in_hbm([qkv_coarse]))
 
     def fine_body(tok_ref, *refs):
         fine_kernel(rows, cols, heads, axes, tok_ref, refs[:4], *refs[4:])
@@ -440,18 +436,35 @@
     )
 
     every = lax.all_to_all(pooled, axes, split_axis=0, concat_axis=0, tiled=True)
+    mine = pl.pallas_call(
+        query_kernel,
+        out_shape=pltpu.HBM((8, width_c), F32),
+        in_specs=vmem(4) + anywhere(1),
+        out_specs=anywhere(1)[0],
+        scratch_shapes=[
+            pltpu.VMEM((width_c, width_c), BF),
+            pltpu.VMEM((8, width_c), F32),
+            pltpu.SemaphoreType.DMA((1,)),
+            pltpu.SemaphoreType.DMA((1,)),
+        ],
+        compiler_params=params,
+        cost_estimate=pl.CostEstimate(
+            flops=2 * width * width_c * width_c, bytes_accessed=6 * MIB, transcendentals=0
+        ),
+        name="query",
+    )(*in_vmem([pooled, up_v, gain_c_v, scale_c_v]), *in_hbm([qkv_coarse]))
     coarse_out, fine = pl.pallas_call(
-        functools.partial(coarse_kernel, axes),
+        coarse_kernel,
         out_shape=[
             jax.ShapeDtypeStruct((1, width_c), BF),
             jax.ShapeDtypeStruct((count, width), BF),
         ],
-        in_specs=vmem(7),
+        in_specs=vmem(5) + anywhere(1),
         out_specs=vmem(1) + anywhere(1),
-        scratch_shapes=[pltpu.VMEM((devices, width_c), F32)] * 2 + [pltpu.SemaphoreType.DMA((1,))],
+        scratch_shapes=[pltpu.VMEM((8, width_c), F32), pltpu.SemaphoreType.DMA((2,))],
         compiler_params=params,
         name="coarse",
-    )(*in_vmem([every, up_v, merged_query, merged, scale_lanes, out_c_v, fine]))
+    )(*in_vmem([every, up_v, merged, out_c_v, fine]), *in_hbm([mine]))
     return fine.reshape(rows, cols, width), coarse_out.reshape(1, 1, width_c)
 
 

time: 32.4 us -> 35.7 us (1.10)
  blocking collectives: 9.77 us -> 0 us
  Pallas kernels: 11.6 us -> 15.5 us
  starting transfers between devices: 10.2 us -> 13.3 us
  local copies, waits for them, and re-layouts: 0 us -> 2.91 us
  waiting for transfers between devices: 0.01 us -> 2.81 us
    all_to_all x1 -> x0, blocking collectives: 9.77 us -> none  [shards(): lax.all_to_all(pooled, axes, split_axis=0, concat_axis=0, tiled=True)]
    pallas_call x1 -> x2, Pallas kernels: 1.67 us -> 6.72 us  [the longest x1 4.48 us: shards(): pl.pallas_call(query_kernel, out_shape=pltpu.HBM((8, width_c), F32), in_s...]
    all_to_all x0 -> x1, starting transfers between devices: none -> 3.1 us  [shards(): lax.all_to_all(pooled, axes, split_axis=0, concat_axis=0, tiled=True)]
    unnamed x0 -> x4, local copies, waits for them, and re-layouts: none -> 2.91 us
    all_to_all x0 -> x1, waiting for transfers between devices: none -> 2.8 us  [shards(): lax.all_to_all(pooled, axes, split_axis=0, concat_axis=0, tiled=True)]
    pallas_call x1, Pallas kernels: 3.98 us -> 2.24 us  [shards(): pl.pallas_call(functools.partial(own_kernel, rows, cols, heads), out_shap...]
    pallas_call x1, Pallas kernels: 1.91 us -> 2.52 us  [shards(): pl.pallas_call(fine_body, out_shape=[pltpu.VMEM((count, width), BF), pltp...]
  transfers between devices with their start and end apart: 4 -> 5, of which waited for: 0 -> 1; matrix products, arithmetic and copies ran while one was open for 0% -> 0% of each run, Pallas kernels for 22% -> 28%
where the time goes in v1:
time: 35.7 us; the launch traced here: 35.2 us
  Pallas kernels  15.5 us (43%)
  starting transfers between devices  13.3 us (37%)
  local copies, waits for them, and re-layouts  2.91 us (8%)
  waiting for transfers between devices  2.81 us (8%)
  between operations  0.74 us (2%)
    ppermute x4, starting transfers between devices, swapped(): return lax.ppermute(array, axis, pairs + [(j, i) for i, j in pairs])  10.1 us
    pallas_call x1, Pallas kernels, shards(): pl.pallas_call(query_kernel, out_shape=pltpu.HBM((8, width_c), F32), in_s...  4.48 us
    all_to_all x1, starting transfers between devices, shards(): lax.all_to_all(pooled, axes, split_axis=0, concat_axis=0, tiled=True)  3.1 us
    pallas_call x1, Pallas kernels, shards(): pl.pallas_call(merge_kernel, out_shape=pltpu.VMEM((width, 2 * width_c), B...  3.02 us
    unnamed x4, local copies, waits for them, and re-layouts  2.91 us
    all_to_all x1, waiting for transfers between devices, shards(): lax.all_to_all(pooled, axes, split_axis=0, concat_axis=0, tiled=True)  2.8 us
    pallas_call x1, Pallas kernels, shards(): pl.pallas_call(fine_body, out_shape=[pltpu.VMEM((count, width), BF), pltp...  2.52 us
    pallas_call x1, Pallas kernels, shards(): pl.pallas_call(functools.partial(own_kernel, rows, cols, heads), out_shap...  2.24 us
  transfers between devices with their start and end apart: 5, of which 1 were waited for; matrix products, arithmetic and copies ran while one was open for 0% of the time, Pallas kernels for 28%

profile of v1, /device:TPU:0, one launch (start us, length us, event | category | flops | bytes accessed | tf_op | source)
XLA Modules:
  0.0 35.2 jit_solution(1125742265039450137)
XLA Ops:
  0.6 0.8 %strips.1 = (bf16[48,256]{1,0:T(8,128)(2,1)S(1)}, bf16[48,256]{1,0:T(8,128)(2,1)S(1)}) custom-call(bf16[256,256]{1,0:T(8,128)(2,1)} %bitcast.8), custom_call_target="tpu_custom_call" | custom-call | tf_op jit(solution)/shard_map/strips/pallas_call | solution.py:358
  1.4 0.7 %collective-permute-start = (bf16[48,256]{1,0:T(8,128)(2,1)S(1)}, bf16[48,256]{1,0:T(8,128)(2,1)S(1)}, u32[]{:S(2)}, u32[]{:S(2)}) collective-permute-start(bf16[48,256]{1,0:T(8,128)(2,1)S(1)} %get-tuple-element.25), channel_id=1, source_target_pairs={{4,8},{12,16},{20,24},{8,4},{16,12},{24,20},{5,9},{13,17},{21,25},... | collective-permute-start | bytes 73736 | tf_op jit(solution)/shard_map/ppermute | solution.py:355
  2.1 4.4 %collective-permute-start.1 = (bf16[48,256]{1,0:T(8,128)(2,1)S(1)}, bf16[48,256]{1,0:T(8,128)(2,1)S(1)}, u32[]{:S(2)}, u32[]{:S(2)}) collective-permute-start(bf16[48,256]{1,0:T(8,128)(2,1)S(1)} %get-tuple-element.26), channel_id=1, source_target_pairs={{0,4},{8,12},{16,20},{24,28},{4,0},{12,8},{20,16},{28,24},{1,5},{9... | collective-permute-start | bytes 73736 | tf_op jit(solution)/shard_map/ppermute | solution.py:355
  6.5 2.2 %own.1 = (bf16[256,256]{1,0:T(8,128)(2,1)S(1)}, bf16[256,768]{1,0:T(8,128)(2,1)S(1)}, f32[1,256]{1,0:T(1,128)S(1)}, f32[1,4]{1,0:T(1,128)S(1)}, bf16[256,1024]{1...) custom-call(bf16[256,256]{1,0:T(8,128)(2,1)} %bitcast.9, ...), custom_call_target="tpu_custom_call" | custom-call | flops 167772160 | bytes 4194304 | tf_op jit(solution)/shard_map/own/pallas_call | solution.py:375
  8.7 0.0 collective-permute-done.across_ref.refs_0_
  8.7 0.0 collective-permute-done.1.within_ref.refs_1_
  8.7 0.2 edges.1
  8.9 0.7 %collective-permute-start.2 = (bf16[80,256]{1,0:T(8,128)(2,1)S(1)}, bf16[80,256]{1,0:T(8,128)(2,1)S(1)}, u32[]{:S(2)}, u32[]{:S(2)}) collective-permute-start(bf16[80,256]{1,0:T(8,128)(2,1)S(1)} %get-tuple-element.28), channel_id=1, source_target_pairs={{1,2},{2,1},{5,6},{6,5},{9,10},{10,9},{13,14},{14,13},{17,18},{18,... | collective-permute-start | bytes 122888 | tf_op jit(solution)/shard_map/ppermute | solution.py:355
  9.6 4.5 %collective-permute-start.3 = (bf16[80,256]{1,0:T(8,128)(2,1)S(1)}, bf16[80,256]{1,0:T(8,128)(2,1)S(1)}, u32[]{:S(2)}, u32[]{:S(2)}) collective-permute-start(bf16[80,256]{1,0:T(8,128)(2,1)S(1)} %get-tuple-element.29.after_ref), channel_id=1, source_target_pairs={{0,1},{2,3},{1,0},{3,2},{4,5},{6,7},{5,4},{7,6},{8,9},{10,11},{9,8... | collective-permute-start | bytes 122888 | tf_op jit(solution)/shard_map/ppermute | solution.py:355
  14.1 3.0 %merge.1.refs_13_.merged_ref = bf16[256,2048]{1,0:T(8,128)(2,1)S(1)} custom-call(bf16[80,256]{1,0:T(8,128)(2,1)S(1)} %get-tuple-element.29.after_ref, bf16[256,1024]{1,0:T(8,128)(2,1)S(1)} %get-tuple-element.38.up_ref, f32[1,1024]{1,0:T(1,128)S(1)} %get-tuple-element.39.gain_ref, bf16[1024,3072]{1,0:T(8,128)(2,1)} %qkv_hbm.3), custom_call_target="tpu_custom_call" | custom-call | flops 1073741824 | bytes 6291456 | tf_op jit(solution)/shard_map/merge/pallas_call | solution.py:402
  17.1 0.0 collective-permute-done.2.refs_2_
  17.1 0.0 collective-permute-done.3.refs_3_
  17.1 2.5 %fine.1 = (bf16[256,256]{1,0:T(8,128)(2,1)S(1)}, f32[32,2,128]{2,1,0:T(2,128)}, bf16[1024,1024]{1,0:T(8,128)(2,1)S(1)}) custom-call(bf16[256,256]{1,0:T(8,128)(2,1)S(1)} %get-tuple-element.24.tok_ref, bf16[48,256]{1,0:T(8,128)(2,1)S(1)} %collective-permute-done.across_ref.refs_0_, bf16[48,256]{1,0:T(8,128)(2,1)S(1)} %collective-permute-done.1.within_ref.refs_1_, ...), custom_call_target="tpu_custom_call" | custom-call | tf_op jit(solution)/shard_map/fine/pallas_call | solution.py:418
  19.6 0.0 copy-start
  19.7 1.3 %copy-done = bf16[1024,1024]{1,0:T(8,128)(2,1)} copy-done((bf16[1024,1024]{1,0:T(8,128)(2,1)}, bf16[1024,1024]{1,0:T(8,128)(2,1)S(1)}, u32[]{:S(2)}) %copy-start) | copy-done | bytes 2097176
  21.0 3.1 %all-to-all-start = ((f32[32,2,128]{2,1,0:T(2,128)}), f32[32,2,128]{2,1,0:T(2,128)S(1)}, u32[]{:S(2)}, u32[]{:S(2)}) async-start(f32[32,2,128]{2,1,0:T(2,128)} %get-tuple-element.40.pooled_ref), calls=%async_computation | async-start | bytes 65536 | tf_op jit(solution)/shard_map/all_to_all | solution.py:438
  24.1 4.5 %query.1.rows_hbm = f32[8,1024]{1,0:T(8,128)} custom-call(f32[32,2,128]{2,1,0:T(2,128)} %get-tuple-element.40.pooled_ref, bf16[256,1024]{1,0:T(8,128)(2,1)S(1)} %get-tuple-element.38.up_ref, f32[1,1024]{1,0:T(1,128)S(1)} %get-tuple-element.39.gain_ref, f32[1,16]{1,0:T(1,128)S(1)} %get-tuple-element.43.scale_ref, bf16[1024,3072]{1,0:T(8,128)(2,1)} %qkv_hbm.3), custom_call_target="tpu_custom_call" | custom-call | flops 536870912 | bytes 6291456 | tf_op jit(solution)/shard_map/query/pallas_call | solution.py:439
  28.6 2.8 %all-to-all-done.pooled_ref = f32[32,2,128]{2,1,0:T(2,128)S(1)} async-done(((f32[32,2,128]{2,1,0:T(2,128)}), f32[32,2,128]{2,1,0:T(2,128)S(1)}, u32[]{:S(2)}, u32[]{:S(2)}) %all-to-all-start) | async-done | bytes 32800 | tf_op jit(solution)/shard_map/all_to_all | solution.py:438
  31.4 0.0 copy-start.1
  31.4 1.6 %copy-done.1 = bf16[1024,1024]{1,0:T(8,128)(2,1)S(1)} copy-done((bf16[1024,1024]{1,0:T(8,128)(2,1)S(1)}, bf16[1024,1024]{1,0:T(8,128)(2,1)}, u32[]{:S(2)}) %copy-start.1) | copy-done | bytes 2097176
  33.0 2.2 %coarse.1 = (bf16[1,1024]{1,0:T(2,128)(2,1)}, bf16[256,256]{1,0:T(8,128)(2,1)}) custom-call(f32[32,2,128]{2,1,0:T(2,128)S(1)} %all-to-all-done.pooled_ref, bf16[256,1024]{1,0:T(8,128)(2,1)S(1)} %get-tuple-element.38.up_ref, bf16[256,2048]{1,0:T(8,128)(2,1)S(1)} %merge.1.refs_13_.merged_ref, bf16[1024,1024]{1,0:T(8,128)(2,1)S(1)} %copy-done.1, ...), custom_call_target="tpu_custom_call" | custom-call | tf_op jit(solution)/shard_map/coarse/pallas_call | solution.py:456
Async XLA Ops:
  1.4 7.3 %collective-permute-start = (bf16[48,256]{1,0:T(8,128)(2,1)S(1)}, bf16[48,256]{1,0:T(8,128)(2,1)S(1)}, u32[]{:S(2)}, u32[]{:S(2)}) collective-permute-start(bf16[48,256]{1,0:T(8,128)(2,1)S(1)} %get-tuple-element.25), channel_id=1, source_target_pairs={{4,8},{12,16},{20,24},{8,4},{16,12},{24,20},{5,9},{13,17},{21,25},... | collective-permute-start | bytes 73736 | tf_op jit(solution)/shard_map/ppermute | solution.py:355
  2.1 6.6 %collective-permute-start.1 = (bf16[48,256]{1,0:T(8,128)(2,1)S(1)}, bf16[48,256]{1,0:T(8,128)(2,1)S(1)}, u32[]{:S(2)}, u32[]{:S(2)}) collective-permute-start(bf16[48,256]{1,0:T(8,128)(2,1)S(1)} %get-tuple-element.26), channel_id=1, source_target_pairs={{0,4},{8,12},{16,20},{24,28},{4,0},{12,8},{20,16},{28,24},{1,5},{9... | collective-permute-start | bytes 73736 | tf_op jit(solution)/shard_map/ppermute | solution.py:355
  8.9 8.2 %collective-permute-start.2 = (bf16[80,256]{1,0:T(8,128)(2,1)S(1)}, bf16[80,256]{1,0:T(8,128)(2,1)S(1)}, u32[]{:S(2)}, u32[]{:S(2)}) collective-permute-start(bf16[80,256]{1,0:T(8,128)(2,1)S(1)} %get-tuple-element.28), channel_id=1, source_target_pairs={{1,2},{2,1},{5,6},{6,5},{9,10},{10,9},{13,14},{14,13},{17,18},{18,... | collective-permute-start | bytes 122888 | tf_op jit(solution)/shard_map/ppermute | solution.py:355
  9.6 7.5 %collective-permute-start.3 = (bf16[80,256]{1,0:T(8,128)(2,1)S(1)}, bf16[80,256]{1,0:T(8,128)(2,1)S(1)}, u32[]{:S(2)}, u32[]{:S(2)}) collective-permute-start(bf16[80,256]{1,0:T(8,128)(2,1)S(1)} %get-tuple-element.29.after_ref), channel_id=1, source_target_pairs={{0,1},{2,3},{1,0},{3,2},{4,5},{6,7},{5,4},{7,6},{8,9},{10,11},{9,8... | collective-permute-start | bytes 122888 | tf_op jit(solution)/shard_map/ppermute | solution.py:355
  19.6 1.3 %copy-start = (bf16[1024,1024]{1,0:T(8,128)(2,1)}, bf16[1024,1024]{1,0:T(8,128)(2,1)S(1)}, u32[]{:S(2)}) copy-start(bf16[1024,1024]{1,0:T(8,128)(2,1)S(1)} %get-tuple-element.41.out_ref) | copy-start | bytes 6291460
  21.0 10.4 %all-to-all-start = ((f32[32,2,128]{2,1,0:T(2,128)}), f32[32,2,128]{2,1,0:T(2,128)S(1)}, u32[]{:S(2)}, u32[]{:S(2)}) async-start(f32[32,2,128]{2,1,0:T(2,128)} %get-tuple-element.40.pooled_ref), calls=%async_computation | async-start | bytes 65536 | tf_op jit(solution)/shard_map/all_to_all | solution.py:438
  31.4 1.6 %copy-start.1 = (bf16[1024,1024]{1,0:T(8,128)(2,1)S(1)}, bf16[1024,1024]{1,0:T(8,128)(2,1)}, u32[]{:S(2)}) copy-start(bf16[1024,1024]{1,0:T(8,128)(2,1)} %copy-done) | copy-start | bytes 6291460
